TPU v7x, 32 devices: a whole 2x2x4 slice. The times are simulated.
32 devices in a mesh: phase: 4 (over x, core), seq: 8 (over z, y).
Axes of the slice: x: 2, y: 2, z: 4, core: 2. Of those that a mesh axis runs over, the one named last changes fastest.
Arguments:
- frames: bfloat16 [4, 1280, 1024], P('phase', 'seq'), may hold values from -6 to 6
- lengths: int32 [4, 8], P('phase'), may hold values from 1 to 640, 1280 in all within a row
- w_query: bfloat16 [4, 1024, 1024], P('phase', None, 'seq'), may hold values from -1 to 1
- w_key: bfloat16 [4, 1024, 1024], P('phase', None, 'seq'), may hold values from -1 to 1
- w_value: bfloat16 [4, 1024, 1024], P('phase', None, 'seq'), may hold values from -0.1875 to 0.1875
- w_output: bfloat16 [4, 1024, 1024], P('phase', None, 'seq'), may hold values from -0.1875 to 0.1875
- conv_in: bfloat16 [4, 1024, 2048], P('phase', None, 'seq'), may hold values from -0.1875 to 0.1875
- conv_taps: bfloat16 [4, 31, 1024], P('phase'), may hold values from -1 to 1
- conv_out: bfloat16 [4, 1024, 1024], P('phase', None, 'seq'), may hold values from -0.1875 to 0.1875
Outputs:
- handed: bfloat16 [4, 1280, 1024], P('phase', 'seq')
Inputs may be any that keep to these rules, and one draw needn't show every extreme that they name: Each phase's lengths sum to 1280 and the largest equals 640.
All inputs are finite; a program needn't handle non-finite values.
Results may differ from a plain program's by a relative error of at most 0.0085.
Values may be sent and summed in bfloat16 or wider, within the bound.
A program may use at most 64 MiB of HBM per device.

v0:
```python
import math
import jax
import jax.numpy as jnp
from jax import lax
from jax.sharding import PartitionSpec as P

HEADS = 16
KERNEL = 31


def padded_2(block, sides, width):
    for axis, dim in sides:
        count = lax.axis_size(axis)
        forward = [(i, i + 1) for i in range(count - 1)]
        backward = [(target, source) for source, target in forward]
        low = lax.ppermute(
            lax.slice_in_dim(block, block.shape[dim] - width, None, axis=dim), axis, forward
        )
        high = lax.ppermute(lax.slice_in_dim(block, 0, width, axis=dim), axis, backward)
        block = jnp.concatenate([low, block, high], axis=dim)
    return block


def passed_along(block, axis, distance):
    devices = range(lax.axis_size(axis))
    route = [((i - distance) % len(devices), i) for i in devices]
    return lax.ppermute(block, axis, route)


def layer_norm(values):
    centre = values - jnp.mean(values, axis=-1, keepdims=True)
    spread = jnp.mean(centre * centre, axis=-1, keepdims=True)
    return centre * lax.rsqrt(spread + 1e-05)


def segment_ids(positions, lengths):
    bounds = jnp.cumsum(lengths)
    return jnp.sum((positions[:, None] >= bounds[None, :]).astype(jnp.int32), axis=1)


def body(frames, lengths, w_query, w_key, w_value, w_output, conv_in, conv_taps, conv_out):
    hidden = frames[0]
    utt_lengths = lengths[0]
    shards = lax.axis_size("seq")
    my_index = lax.axis_index("seq")
    local_rows = hidden.shape[0]
    width = hidden.shape[1]
    total_rows = local_rows * shards
    head_size = width // HEADS
    scale = 1.0 / math.sqrt(head_size)
    groups = min(HEADS, shards)
    group_heads = HEADS // groups
    parts = shards // groups
    part_rows = local_rows // parts
    group_width = group_heads * head_size
    full_query, full_key, full_value, full_output, full_conv_in, full_conv_out = (
        lax.all_gather(w_query[0], "seq", axis=1, tiled=True),
        lax.all_gather(w_key[0], "seq", axis=1, tiled=True),
        lax.all_gather(w_value[0], "seq", axis=1, tiled=True),
        lax.all_gather(w_output[0], "seq", axis=1, tiled=True),
        lax.all_gather(conv_in[0], "seq", axis=1, tiled=True),
        lax.all_gather(conv_out[0], "seq", axis=1, tiled=True),
    )
    normed = layer_norm(hidden.astype(jnp.float32)).astype(jnp.bfloat16)
    query = jnp.dot(normed, full_query, preferred_element_type=jnp.float32).astype(jnp.bfloat16)
    key_proj = jnp.dot(normed, full_key, preferred_element_type=jnp.float32).astype(jnp.bfloat16)
    value_proj = jnp.dot(normed, full_value, preferred_element_type=jnp.float32).astype(
        jnp.bfloat16
    )
    shaped = query.reshape(parts, part_rows, groups, group_width).transpose(2, 0, 1, 3)
    query_pieces = shaped.reshape(shards, part_rows, group_width)
    kv_local = jnp.concatenate(
        [
            key_proj.reshape(local_rows, groups, group_width),
            value_proj.reshape(local_rows, groups, group_width),
        ],
        axis=2,
    )
    copies = jnp.broadcast_to(
        kv_local.transpose(1, 0, 2)[:, None], (groups, parts, local_rows, 2 * group_width)
    )
    copies = copies.reshape(shards, local_rows, 2 * group_width)
    query_got, kv_got = (
        lax.all_to_all(query_pieces, "seq", split_axis=0, concat_axis=0, tiled=True),
        lax.all_to_all(copies, "seq", split_axis=0, concat_axis=0, tiled=True),
    )
    key_value = kv_got.reshape(total_rows, 2 * group_width)
    count = shards * part_rows
    my_part = my_index % parts
    row_ids = jnp.arange(count, dtype=jnp.int32)
    query_pos = row_ids // part_rows * local_rows + my_part * part_rows + row_ids % part_rows
    queries = query_got.reshape(count, group_heads, head_size)
    key_rows = key_value[:, :group_width].reshape(total_rows, group_heads, head_size)
    value_rows = key_value[:, group_width:].reshape(total_rows, group_heads, head_size)
    seg_all = segment_ids(jnp.arange(total_rows, dtype=jnp.int32), utt_lengths)
    seg_query = segment_ids(query_pos, utt_lengths)
    query_block = math.gcd(512, count)
    blocks = count // query_block

    def attend_block(operands):
        block_query, block_seg = operands
        scores = (
            jnp.einsum("qhd,khd->hqk", block_query, key_rows, preferred_element_type=jnp.float32)
            * scale
        )
        allowed = (block_seg[:, None] == seg_all[None, :])[None]
        scores = jnp.where(allowed, scores, -1e30)
        peak = jnp.max(scores, axis=2, keepdims=True)
        expw = jnp.where(allowed, jnp.exp(scores - peak), 0.0)
        total_weight = jnp.sum(expw, axis=2)
        mixed = jnp.einsum(
            "hqk,khd->hqd",
            expw.astype(jnp.bfloat16),
            value_rows,
            preferred_element_type=jnp.float32,
        )
        mixed = mixed / total_weight[:, :, None]
        return mixed.transpose(1, 0, 2).astype(jnp.bfloat16)

    attended = lax.map(
        attend_block,
        (
            queries.reshape(blocks, query_block, group_heads, head_size),
            seg_query.reshape(blocks, query_block),
        ),
    )
    outgoing = attended.reshape(shards, part_rows, group_width)
    returned = lax.all_to_all(outgoing, "seq", split_axis=0, concat_axis=0, tiled=True)
    attended_local = (
        returned.reshape(groups, parts, part_rows, group_width)
        .transpose(1, 2, 0, 3)
        .reshape(local_rows, width)
    )
    after_attn = hidden.astype(jnp.float32) + jnp.dot(
        attended_local, full_output, preferred_element_type=jnp.float32
    )
    conv_normed = layer_norm(after_attn).astype(jnp.bfloat16)
    gates = jnp.dot(conv_normed, full_conv_in, preferred_element_type=jnp.float32)
    glu = (gates[:, :width] * jax.nn.sigmoid(gates[:, width:])).astype(jnp.bfloat16)
    reach = KERNEL // 2
    padded = padded_2(glu, (("seq", 0),), KERNEL // 2)
    padded_pos = my_index * local_rows - reach + jnp.arange(local_rows + 2 * reach, dtype=jnp.int32)
    inside = (padded_pos >= 0) & (padded_pos < total_rows)
    padded_seg = jnp.where(inside, segment_ids(padded_pos, utt_lengths), -1)
    own_seg = padded_seg[reach : reach + local_rows]
    taps = conv_taps[0]
    depthwise = jnp.zeros((local_rows, width), jnp.float32)
    for offset in range(KERNEL):
        keep = padded_seg[offset : offset + local_rows] == own_seg
        term = padded[offset : offset + local_rows].astype(jnp.float32) * taps[offset].astype(
            jnp.float32
        )
        depthwise = depthwise + jnp.where(keep[:, None], term, 0.0)
    conv_act = layer_norm(depthwise)
    conv_act = (conv_act * jax.nn.sigmoid(conv_act)).astype(jnp.bfloat16)
    block_out = (
        after_attn + jnp.dot(conv_act, full_conv_out, preferred_element_type=jnp.float32)
    ).astype(jnp.bfloat16)
    passed = passed_along(block_out, "phase", 1)
    return passed[None]


def solution(mesh):
    in_specs = (
        P("phase", "seq", None),
        P("phase", None),
        P("phase", None, "seq"),
        P("phase", None, "seq"),
        P("phase", None, "seq"),
        P("phase", None, "seq"),
        P("phase", None, "seq"),
        P("phase", None, None),
        P("phase", None, "seq"),
    )
    out_specs = P("phase", "seq", None)
    return jax.shard_map(body, mesh=mesh, in_specs=in_specs, out_specs=out_specs, check_vma=False)
```

profile of v0, /device:TPU:0, one launch (start us, length us, event | category | flops | bytes accessed | tf_op | source)
XLA Modules:
  0.0 378.4 jit_solution(5348660452825907800)
XLA Ops:
  12.3 50.9 %all-gather.13.cloned.1.call-done = bf16[1,1024,1024]{2,1,0:T(8,128)(2,1)} async-done(((bf16[1,1024,128]{2,1,0:T(8,128)(2,1)}), bf16[1,1024,1024]{2,1,0:T(8,128)(2,1)}) %all-gather.13.cloned.1.call-update) | async-done | bytes 2097168 | tf_op jit(solution)/shard_map/all_gather | solution.py:57
  66.3 3.4 all-to-all-start
  69.8 47.7 %all-gather.17.cloned.1.call-done = bf16[1,1024,1024]{2,1,0:T(8,128)(2,1)} async-done(((bf16[1,1024,128]{2,1,0:T(8,128)(2,1)}), bf16[1,1024,1024]{2,1,0:T(8,128)(2,1)}) %all-gather.17.cloned.1.call-update) | async-done | bytes 2097168 | tf_op jit(solution)/shard_map/all_gather | solution.py:59
  119.7 49.1 %all-gather.15.cloned.1.call-done = bf16[1,1024,1024]{2,1,0:T(8,128)(2,1)} async-done(((bf16[1,1024,128]{2,1,0:T(8,128)(2,1)}), bf16[1,1024,1024]{2,1,0:T(8,128)(2,1)}) %all-gather.15.cloned.1.call-update) | async-done | bytes 2097168 | tf_op jit(solution)/shard_map/all_gather | solution.py:58
  172.0 3.5 all-to-all-start.1
  178.2 22.7 %all-to-all-done.1 = bf16[8,160,256]{2,1,0:T(8,128)(2,1)S(1)} async-done(((bf16[8,160,256]{2,1,0:T(8,128)(2,1)}), bf16[8,160,256]{2,1,0:T(8,128)(2,1)S(1)}, u32[]{:S(2)}, u32[]{:S(2)}) %all-to-all-start.1) | async-done | bytes 655392 | tf_op jit(solution)/shard_map/all_to_all | solution.py:85
  202.8 33.4 %while.10 = (s32[]{:T(128)}, bf16[5,256,2,64]{1,3,2,0:T(8,128)(2,1)}, s32[5,256]{1,0:T(8,128)S(1)}, s32[1280]{0:T(1024)S(1)}, bf16[5,256,2,64]{1,3,2,0:T(8,128)(...) while((s32[]{:T(128)}, bf16[5,256,2,64]{1,3,2,0:T(8,128)(2,1)}, ...), condition=%wide.region_8.9_spmd, body=%wide.region_5.8_spmd.sunk | while | flops 258608128 | bytes 10696281 | solution.py:120
  204.7 2.4 fusion.161
  207.2 2.3 fusion.162
  211.4 2.4 fusion.161
  213.8 2.3 fusion.162
  218.1 2.4 fusion.161
  220.5 2.3 fusion.162
  224.7 2.4 fusion.161
  231.4 2.4 fusion.161
  238.6 3.6 all-to-all-start.2
  242.4 15.6 %all-to-all-done.2 = bf16[8,160,128]{2,1,0:T(8,128)(2,1)S(1)} async-done(((bf16[8,160,128]{2,1,0:T(8,128)(2,1)}), bf16[8,160,128]{2,1,0:T(8,128)(2,1)S(1)}, u32[]{:S(2)}, u32[]{:S(2)}) %all-to-all-start.2) | async-done | bytes 327712 | tf_op jit(solution)/shard_map/all_to_all | solution.py:128
  260.7 50.0 %all-gather.21.cloned.1.call-done = bf16[1,1024,2048]{2,1,0:T(8,128)(2,1)} async-done(((bf16[1,1024,256]{2,1,0:T(8,128)(2,1)}), bf16[1,1024,2048]{2,1,0:T(8,128)(2,1)}) %all-gather.21.cloned.1.call-update) | async-done | bytes 4194320 | tf_op jit(solution)/shard_map/all_gather | solution.py:61
  310.7 3.1 fusion.35
  314.0 3.4 collective-permute-start
  319.0 4.7 %collective-permute-done.1 = bf16[15,1024]{1,0:T(8,128)(2,1)S(1)} collective-permute-done((bf16[15,1024]{1,0:T(8,128)(2,1)S(1)}, bf16[15,1024]{1,0:T(8,128)(2,1)S(1)}, u32[]{:S(2)}, u32[]{:S(2)}) %collective-permute-start.1) | collective-permute-done | bytes 30752 | tf_op jit(solution)/shard_map/ppermute | solution.py:19
  323.7 4.1 %fusion.132 = (f32[160]{0:T(256)S(1)}, f32[160,1024]{1,0:T(8,128)S(1)}) fusion(f32[1024]{0:T(1024)S(1)} %bitcast.191, bf16[15,1024]{1,0:T(8,128)(2,1)S(1)} %collective-permute-done.1, bf16[160,1024]{1,0:T(8,128)(2,1)S(1)} %fusion.83, pred[160]{0:T(512)(128)(4,1)S(1)} %get-tuple-element.146, f32[1024]{0:T(1024)S(1)} %bitcast.192, ...), kind=kLoop, calls=%fused_computation.239 | loop fusion | flops 34897760 | bytes 1176896 | tf_op jit(solution)/shard_map/reduce_sum | solution.py:31
  328.0 34.0 %all-gather.23.cloned.1.call-done = bf16[1,1024,1024]{2,1,0:T(8,128)(2,1)} async-done(((bf16[1,1024,128]{2,1,0:T(8,128)(2,1)}), bf16[1,1024,1024]{2,1,0:T(8,128)(2,1)}) %all-gather.23.cloned.1.call-update) | async-done | bytes 2097168 | tf_op jit(solution)/shard_map/all_gather | solution.py:62
  364.3 6.5 %collective-permute-done.2 = bf16[160,1024]{1,0:T(8,128)(2,1)S(1)} collective-permute-done((bf16[160,1024]{1,0:T(8,128)(2,1)S(1)}, bf16[160,1024]{1,0:T(8,128)(2,1)S(1)}, u32[]{:S(2)}, u32[]{:S(2)}) %collective-permute-start.2) | collective-permute-done | bytes 327712 | tf_op jit(solution)/shard_map/ppermute | solution.py:27
  (85 shorter events, 43.0 us)
Async XLA Ops:
  6.5 56.7 %all-gather.13.cloned.1.call-start = ((), (), s32[]{:S(2)}) async-start(), calls=%async_computation.3 | async-start | bytes 2359296 | tf_op jit(solution)/shard_map/all_gather | solution.py:57
  7.3 110.2 %all-gather.17.cloned.1.call-start = ((), (), s32[]{:S(2)}) async-start(), calls=%async_computation.5 | async-start | bytes 2359296 | tf_op jit(solution)/shard_map/all_gather | solution.py:59
  8.0 160.8 %all-gather.15.cloned.1.call-start = ((), (), s32[]{:S(2)}) async-start(), calls=%async_computation.4 | async-start | bytes 2359296 | tf_op jit(solution)/shard_map/all_gather | solution.py:58
  8.7 249.5 %all-gather.19.cloned.1.call-start = ((), (), s32[]{:S(2)}) async-start(), calls=%async_computation.6 | async-start | bytes 2359296 | tf_op jit(solution)/shard_map/all_gather | solution.py:60
  9.3 301.4 %all-gather.21.cloned.1.call-start = ((), (), s32[]{:S(2)}) async-start(), calls=%async_computation.7 | async-start | bytes 4718592 | tf_op jit(solution)/shard_map/all_gather | solution.py:61
  9.9 107.6 %copy-start = (bf16[1,160,1024]{2,1,0:T(8,128)(2,1)S(1)}, bf16[1,160,1024]{2,1,0:T(8,128)(2,1)}, u32[]{:S(2)}) copy-start(bf16[1,160,1024]{2,1,0:T(8,128)(2,1)} %param.11) | copy-start | bytes 983044
  66.3 105.7 %all-to-all-start = ((bf16[8,160,128]{2,1,0:T(8,128)(2,1)}), bf16[8,160,128]{2,1,0:T(8,128)(2,1)S(1)}, u32[]{:S(2)}, u32[]{:S(2)}) async-start(bf16[8,160,128]{2,1,0:T(8,128)(2,1)} %bitcast.150), calls=%async_computation | async-start | bytes 655360 | tf_op jit(solution)/shard_map/all_to_all | solution.py:84
  119.7 56.4 %copy-start.2 = (s32[1,8]{1,0:T(1,128)S(1)}, s32[1,8]{1,0:T(1,128)}, u32[]{:S(2)}) copy-start(s32[1,8]{1,0:T(1,128)} %param.12) | copy-start | bytes 100
  119.7 57.0 %copy-start.1 = (bf16[1,31,1024]{2,1,0:T(8,128)(2,1)S(1)}, bf16[1,31,1024]{2,1,0:T(8,128)(2,1)}, u32[]{:S(2)}) copy-start(bf16[1,31,1024]{2,1,0:T(8,128)(2,1)} %param.18) | copy-start | bytes 190468
  172.0 28.9 %all-to-all-start.1 = ((bf16[8,160,256]{2,1,0:T(8,128)(2,1)}), bf16[8,160,256]{2,1,0:T(8,128)(2,1)S(1)}, u32[]{:S(2)}, u32[]{:S(2)}) async-start(bf16[8,160,256]{2,1,0:T(8,128)(2,1)} %maximum_bitcast_fusion), calls=%async_computation.1 | async-start | bytes 1310720 | tf_op jit(solution)/shard_map/all_to_all | solution.py:85
  175.5 186.5 %all-gather.23.cloned.1.call-start = ((), (), s32[]{:S(2)}) async-start(), calls=%async_computation.8 | async-start | bytes 2359296 | tf_op jit(solution)/shard_map/all_gather | solution.py:62
  238.6 19.5 %all-to-all-start.2 = ((bf16[8,160,128]{2,1,0:T(8,128)(2,1)}), bf16[8,160,128]{2,1,0:T(8,128)(2,1)S(1)}, u32[]{:S(2)}, u32[]{:S(2)}) async-start(bf16[8,160,128]{2,1,0:T(8,128)(2,1)} %reshape.468), calls=%async_computation.2 | async-start | bytes 655360 | tf_op jit(solution)/shard_map/all_to_all | solution.py:128
  314.0 5.0 %collective-permute-start = (bf16[15,1024]{1,0:T(8,128)(2,1)S(1)}, bf16[15,1024]{1,0:T(8,128)(2,1)S(1)}, u32[]{:S(2)}, u32[]{:S(2)}) collective-permute-start(bf16[15,1024]{1,0:T(8,128)(2,1)S(1)} %get-tuple-element.84), channel_id=1, source_target_pairs={{0,1},{1,2},{2,3},{3,4},{4,5},{5,6},{6,7},{8,9},{9,10},{10,11},{11... | collective-permute-start | bytes 92168 | tf_op jit(solution)/shard_map/ppermute | solution.py:16
  317.4 6.3 %collective-permute-start.1 = (bf16[15,1024]{1,0:T(8,128)(2,1)S(1)}, bf16[15,1024]{1,0:T(8,128)(2,1)S(1)}, u32[]{:S(2)}, u32[]{:S(2)}) collective-permute-start(bf16[15,1024]{1,0:T(8,128)(2,1)S(1)} %get-tuple-element.85), channel_id=1, source_target_pairs={{1,0},{2,1},{3,2},{4,3},{5,4},{6,5},{7,6},{9,8},{10,9},{11,10},{12... | collective-permute-start | bytes 92168 | tf_op jit(solution)/shard_map/ppermute | solution.py:19
  364.2 6.6 %collective-permute-start.2 = (bf16[160,1024]{1,0:T(8,128)(2,1)S(1)}, bf16[160,1024]{1,0:T(8,128)(2,1)S(1)}, u32[]{:S(2)}, u32[]{:S(2)}) collective-permute-start(bf16[160,1024]{1,0:T(8,128)(2,1)S(1)} %fusion.53), channel_id=1, source_target_pairs={{24,0},{0,8},{8,16},{16,24},{25,1},{1,9},{9,17},{17,25},{26,2},{2,... | collective-permute-start | bytes 983048 | tf_op jit(solution)/shard_map/ppermute | solution.py:27
Sparse Core Ops, SparseCore 0:
  9.4 53.7 all-gather.12
  65.2 52.1 all-gather.16
  119.5 49.2 all-gather.14
  170.7 57.7 all-gather.18
  230.4 80.2 all-gather.20
  312.6 49.3 all-gather.22
where the time goes:
time: 379 us; the launch traced here: 378 us
  waiting for transfers between devices  285 us (75%)
  matrix products  46 us (12%)
  starting transfers between devices  15.7 us (4%)
  between operations  13.8 us (4%)
  other arithmetic  10.2 us (3%)
  local copies, waits for them, and re-layouts  7.62 us (2%)
    all_gather x1, waiting for transfers between devices, body(): lax.all_gather(w_query[0], 'seq', axis=1, tiled=True)  50.9 us
    all_gather x1, waiting for transfers between devices, body(): lax.all_gather(conv_in[0], 'seq', axis=1, tiled=True)  50 us
    all_gather x1, waiting for transfers between devices, body(): lax.all_gather(w_key[0], 'seq', axis=1, tiled=True)  49.1 us
    all_gather x1, waiting for transfers between devices, body(): lax.all_gather(w_value[0], 'seq', axis=1, tiled=True)  47.7 us
    all_gather x1, waiting for transfers between devices, body(): lax.all_gather(conv_out[0], 'seq', axis=1, tiled=True)  34 us
    all_to_all x1, waiting for transfers between devices, body(): lax.all_to_all(copies, 'seq', split_axis=0, concat_axis=0, tiled=True)  22.7 us
    all_to_all x1, waiting for transfers between devices, body(): lax.all_to_all(outgoing, 'seq', split_axis=0, concat_axis=0, tiled=True)  15.6 us
    sub x5, matrix products, attend_block(): expw = jnp.where(allowed, jnp.exp(scores - peak), 0.0)  12.2 us
  transfers between devices with their start and end apart: 12, of which 9 were waited for; matrix products, arithmetic and copies ran while one was open for 16% of the time, Pallas kernels for 0%

commit v1 on v0

--- a/solution.py
+++ b/solution.py
@@ -1,3 +1,4 @@
+import functools
 import math
 import jax
 import jax.numpy as jnp
@@ -6,6 +7,46 @@
 
 HEADS = 16
 KERNEL = 31
+
+
+def marks_begin(incoming_x, axis_key):
+    b_next, all_rows, arr_now = (
+        lax.axis_size(axis_key),
+        lax.axis_index(axis_key),
+        incoming_x.shape[1],
+    )
+    leaves = []
+    m = 0
+    while m < b_next:
+        leaves.append((m, (m + 1) % b_next))
+        m = m + 1
+    ledger = []
+    m = 0
+    while m < b_next:
+        ledger.append((m, (m - 1) % b_next))
+        m = m + 1
+    parts_out = jnp.zeros(
+        (*incoming_x.shape[:1], b_next * arr_now, *incoming_x.shape[2:]), incoming_x.dtype
+    )
+    parts_out = lax.dynamic_update_slice_in_dim(parts_out, incoming_x, all_rows * arr_now, axis=1)
+    work_now = arr_next = incoming_x
+    t_next = b_next // 2
+    src_i = 1
+    while src_i < t_next + 1:
+        work_now = lax.ppermute(work_now, axis_key, leaves)
+        parts_out = lax.dynamic_update_slice_in_dim(
+            parts_out, work_now, (all_rows - src_i) % b_next * arr_now, axis=1
+        )
+        if src_i < b_next - t_next:
+            arr_next = lax.ppermute(arr_next, axis_key, ledger)
+            parts_out = lax.dynamic_update_slice_in_dim(
+                parts_out, arr_next, (all_rows + src_i) % b_next * arr_now, axis=1
+            )
+        src_i += 1
+    return parts_out
+
+
+points_hold = functools.partial(marks_begin, axis_key="seq")
 
 
 def padded_2(block, sides, width):
@@ -56,7 +97,7 @@
     full_query, full_key, full_value, full_output, full_conv_in, full_conv_out = (
         lax.all_gather(w_query[0], "seq", axis=1, tiled=True),
         lax.all_gather(w_key[0], "seq", axis=1, tiled=True),
-        lax.all_gather(w_value[0], "seq", axis=1, tiled=True),
+        points_hold(w_value[0]),
         lax.all_gather(w_output[0], "seq", axis=1, tiled=True),
         lax.all_gather(conv_in[0], "seq", axis=1, tiled=True),
         lax.all_gather(conv_out[0], "seq", axis=1, tiled=True),

time: 379 us -> 347 us (0.916)
  waiting for transfers between devices: 285 us -> 238 us
  starting transfers between devices: 15.7 us -> 34 us
    all_gather x1 -> x0, waiting for transfers between devices: 47.7 us -> none  [body(): lax.all_gather(w_value[0], 'seq', axis=1, tiled=True)]
    ppermute x0 -> x7, waiting for transfers between devices: none -> 35.1 us  [the longest x4 25.8 us: marks_begin(): work_now = lax.ppermute(work_now, axis_key, leaves)]
    all_gather x1, waiting for transfers between devices: 50.9 us -> 16.8 us  [body(): lax.all_gather(w_query[0], 'seq', axis=1, tiled=True)]
    ppermute x0 -> x7, starting transfers between devices: none -> 17.9 us  [the longest x3 12.5 us: marks_begin(): arr_next = lax.ppermute(arr_next, axis_key, ledger)]
  transfers between devices with their start and end apart: 12 -> 18, of which waited for: 9 -> 14; matrix products, arithmetic and copies ran while one was open for 16% -> 17% of each run, Pallas kernels for 0% -> 0%
where the time goes in v1:
time: 347 us; the launch traced here: 346 us
  waiting for transfers between devices  238 us (69%)
  matrix products  44.4 us (13%)
  starting transfers between devices  34 us (10%)
  between operations  13.5 us (4%)
  local copies, waits for them, and re-layouts  8.57 us (2%)
  other arithmetic  8.13 us (2%)
    all_gather x1, waiting for transfers between devices, body(): lax.all_gather(conv_in[0], 'seq', axis=1, tiled=True)  50 us
    all_gather x1, waiting for transfers between devices, body(): lax.all_gather(w_key[0], 'seq', axis=1, tiled=True)  49.2 us
    all_gather x1, waiting for transfers between devices, body(): lax.all_gather(conv_out[0], 'seq', axis=1, tiled=True)  34 us
    ppermute x4, waiting for transfers between devices, marks_begin(): work_now = lax.ppermute(work_now, axis_key, leaves)  25.8 us
    all_to_all x1, waiting for transfers between devices, body(): lax.all_to_all(copies, 'seq', split_axis=0, concat_axis=0, tiled=True)  22.7 us
    all_gather x1, waiting for transfers between devices, body(): lax.all_gather(w_query[0], 'seq', axis=1, tiled=True)  16.8 us
    all_to_all x1, waiting for transfers between devices, body(): lax.all_to_all(outgoing, 'seq', split_axis=0, concat_axis=0, tiled=True)  15.6 us
    ppermute x3, starting transfers between devices, marks_begin(): arr_next = lax.ppermute(arr_next, axis_key, ledger)  12.5 us
  transfers between devices with their start and end apart: 18, of which 14 were waited for; matrix products, arithmetic and copies ran while one was open for 17% of the time, Pallas kernels for 0%

profile of v1, /device:TPU:0, one launch (start us, length us, event | category | flops | bytes accessed | tf_op | source)
XLA Modules:
  0.0 346.5 jit_solution(13856027414334923147)
XLA Ops:
  9.3 3.0 collective-permute-start
  12.3 3.1 collective-permute-start.1
  16.0 10.7 %collective-permute-done = bf16[1024,128]{1,0:T(8,128)(2,1)S(1)} collective-permute-done((bf16[1024,128]{1,0:T(8,128)(2,1)}, bf16[1024,128]{1,0:T(8,128)(2,1)S(1)}, u32[]{:S(2)}, u32[]{:S(2)}) %collective-permute-start) | collective-permute-done | bytes 262176 | tf_op jit(solution)/shard_map/ppermute | solution.py:36
  29.3 3.8 %collective-permute-start.3 = (bf16[1024,128]{1,0:T(8,128)(2,1)S(1)}, bf16[1024,128]{1,0:T(8,128)(2,1)S(1)}, u32[]{:S(2)}, u32[]{:S(2)}) collective-permute-start(bf16[1024,128]{1,0:T(8,128)(2,1)S(1)} %collective-permute-done.1), channel_id=1, source_target_pairs={{0,7},{1,0},{2,1},{3,2},{4,3},{5,4},{6,5},{7,6},{8,15},{9,8},{10,9... | collective-permute-start | bytes 786440 | tf_op jit(solution)/shard_map/ppermute | solution.py:41
  33.1 7.6 %collective-permute-done.2 = bf16[1024,128]{1,0:T(8,128)(2,1)S(1)} collective-permute-done((bf16[1024,128]{1,0:T(8,128)(2,1)S(1)}, bf16[1024,128]{1,0:T(8,128)(2,1)S(1)}, u32[]{:S(2)}, u32[]{:S(2)}) %collective-permute-start.2) | collective-permute-done | bytes 262176 | tf_op jit(solution)/shard_map/ppermute | solution.py:36
  41.3 5.6 %collective-permute-start.5 = (bf16[1024,128]{1,0:T(8,128)(2,1)S(1)}, bf16[1024,128]{1,0:T(8,128)(2,1)S(1)}, u32[]{:S(2)}, u32[]{:S(2)}) collective-permute-start(bf16[1024,128]{1,0:T(8,128)(2,1)S(1)} %collective-permute-done.3), channel_id=1, source_target_pairs={{0,7},{1,0},{2,1},{3,2},{4,3},{5,4},{6,5},{7,6},{8,15},{9,8},{10,9... | collective-permute-start | bytes 786440 | tf_op jit(solution)/shard_map/ppermute | solution.py:41
  47.0 2.9 collective-permute-done.4
  50.1 8.9 %collective-permute-done.5 = bf16[1024,128]{1,0:T(8,128)(2,1)S(1)} collective-permute-done((bf16[1024,128]{1,0:T(8,128)(2,1)S(1)}, bf16[1024,128]{1,0:T(8,128)(2,1)S(1)}, u32[]{:S(2)}, u32[]{:S(2)}) %collective-permute-start.5) | collective-permute-done | bytes 262176 | tf_op jit(solution)/shard_map/ppermute | solution.py:41
  59.1 4.6 %collective-permute-done.6 = bf16[1024,128]{1,0:T(8,128)(2,1)S(1)} collective-permute-done((bf16[1024,128]{1,0:T(8,128)(2,1)S(1)}, bf16[1024,128]{1,0:T(8,128)(2,1)S(1)}, u32[]{:S(2)}, u32[]{:S(2)}) %collective-permute-start.6) | collective-permute-done | bytes 262176 | tf_op jit(solution)/shard_map/ppermute | solution.py:36
  63.8 16.8 %all-gather.11.cloned.1.call-done = bf16[1,1024,1024]{2,1,0:T(8,128)(2,1)} async-done(((bf16[1,1024,128]{2,1,0:T(8,128)(2,1)}), bf16[1,1024,1024]{2,1,0:T(8,128)(2,1)}) %all-gather.11.cloned.1.call-update) | async-done | bytes 2097168 | tf_op jit(solution)/shard_map/all_gather | solution.py:98
  83.5 3.9 %all-to-all-start = ((bf16[8,160,128]{2,1,0:T(8,128)(2,1)}), bf16[8,160,128]{2,1,0:T(8,128)(2,1)S(1)}, u32[]{:S(2)}, u32[]{:S(2)}) async-start(bf16[8,160,128]{2,1,0:T(8,128)(2,1)} %bitcast.146), calls=%async_computation | async-start | bytes 655360 | tf_op jit(solution)/shard_map/all_to_all | solution.py:125
  88.0 49.2 %all-gather.13.cloned.1.call-done = bf16[1,1024,1024]{2,1,0:T(8,128)(2,1)} async-done(((bf16[1,1024,128]{2,1,0:T(8,128)(2,1)}), bf16[1,1024,1024]{2,1,0:T(8,128)(2,1)}) %all-gather.13.cloned.1.call-update) | async-done | bytes 2097168 | tf_op jit(solution)/shard_map/all_gather | solution.py:99
  140.4 3.5 %all-to-all-start.1 = ((bf16[8,160,256]{2,1,0:T(8,128)(2,1)}), bf16[8,160,256]{2,1,0:T(8,128)(2,1)S(1)}, u32[]{:S(2)}, u32[]{:S(2)}) async-start(bf16[8,160,256]{2,1,0:T(8,128)(2,1)} %maximum_bitcast_fusion), calls=%async_computation.1 | async-start | bytes 1310720 | tf_op jit(solution)/shard_map/all_to_all | solution.py:126
  146.6 22.7 %all-to-all-done.1 = bf16[8,160,256]{2,1,0:T(8,128)(2,1)S(1)} async-done(((bf16[8,160,256]{2,1,0:T(8,128)(2,1)}), bf16[8,160,256]{2,1,0:T(8,128)(2,1)S(1)}, u32[]{:S(2)}, u32[]{:S(2)}) %all-to-all-start.1) | async-done | bytes 655392 | tf_op jit(solution)/shard_map/all_to_all | solution.py:126
  171.2 33.4 %while.10 = (s32[]{:T(128)}, bf16[5,256,2,64]{1,3,2,0:T(8,128)(2,1)}, s32[5,256]{1,0:T(8,128)S(1)}, s32[1280]{0:T(1024)S(1)}, bf16[5,256,2,64]{1,3,2,0:T(8,128)(...) while((s32[]{:T(128)}, bf16[5,256,2,64]{1,3,2,0:T(8,128)(2,1)}, ...), condition=%wide.region_8.9_spmd, body=%wide.region_5.8_spmd.sunk | while | flops 258608128 | bytes 10696281 | solution.py:161
  207.0 3.6 %all-to-all-start.2 = ((bf16[8,160,128]{2,1,0:T(8,128)(2,1)}), bf16[8,160,128]{2,1,0:T(8,128)(2,1)S(1)}, u32[]{:S(2)}, u32[]{:S(2)}) async-start(bf16[8,160,128]{2,1,0:T(8,128)(2,1)} %reshape.468), calls=%async_computation.2 | async-start | bytes 655360 | tf_op jit(solution)/shard_map/all_to_all | solution.py:169
  210.9 15.6 %all-to-all-done.2 = bf16[8,160,128]{2,1,0:T(8,128)(2,1)S(1)} async-done(((bf16[8,160,128]{2,1,0:T(8,128)(2,1)}), bf16[8,160,128]{2,1,0:T(8,128)(2,1)S(1)}, u32[]{:S(2)}, u32[]{:S(2)}) %all-to-all-start.2) | async-done | bytes 327712 | tf_op jit(solution)/shard_map/all_to_all | solution.py:169
  229.1 50.0 %all-gather.17.cloned.1.call-done = bf16[1,1024,2048]{2,1,0:T(8,128)(2,1)} async-done(((bf16[1,1024,256]{2,1,0:T(8,128)(2,1)}), bf16[1,1024,2048]{2,1,0:T(8,128)(2,1)}) %all-gather.17.cloned.1.call-update) | async-done | bytes 4194320 | tf_op jit(solution)/shard_map/all_gather | solution.py:102
  279.2 3.1 fusion.35
  282.5 3.4 collective-permute-start.7
  287.4 4.7 %collective-permute-done.8 = bf16[15,1024]{1,0:T(8,128)(2,1)S(1)} collective-permute-done((bf16[15,1024]{1,0:T(8,128)(2,1)S(1)}, bf16[15,1024]{1,0:T(8,128)(2,1)S(1)}, u32[]{:S(2)}, u32[]{:S(2)}) %collective-permute-start.8) | collective-permute-done | bytes 30752 | tf_op jit(solution)/shard_map/ppermute | solution.py:60
  292.1 4.1 %fusion.125 = (f32[160]{0:T(256)S(1)}, f32[160,1024]{1,0:T(8,128)S(1)}) fusion(f32[1024]{0:T(1024)S(1)} %bitcast.189, bf16[15,1024]{1,0:T(8,128)(2,1)S(1)} %collective-permute-done.8, bf16[160,1024]{1,0:T(8,128)(2,1)S(1)} %fusion.76, pred[160]{0:T(512)(128)(4,1)S(1)} %get-tuple-element.146, f32[1024]{0:T(1024)S(1)} %bitcast.190, ...), kind=kLoop, calls=%fused_computation.245 | loop fusion | flops 34897760 | bytes 1176896 | tf_op jit(solution)/shard_map/reduce_sum | solution.py:72
  296.5 34.0 %all-gather.19.cloned.1.call-done = bf16[1,1024,1024]{2,1,0:T(8,128)(2,1)} async-done(((bf16[1,1024,128]{2,1,0:T(8,128)(2,1)}), bf16[1,1024,1024]{2,1,0:T(8,128)(2,1)}) %all-gather.19.cloned.1.call-update) | async-done | bytes 2097168 | tf_op jit(solution)/shard_map/all_gather | solution.py:103
  332.7 6.5 %collective-permute-done.9 = bf16[160,1024]{1,0:T(8,128)(2,1)S(1)} collective-permute-done((bf16[160,1024]{1,0:T(8,128)(2,1)S(1)}, bf16[160,1024]{1,0:T(8,128)(2,1)S(1)}, u32[]{:S(2)}, u32[]{:S(2)}) %collective-permute-start.9) | collective-permute-done | bytes 327712 | tf_op jit(solution)/shard_map/ppermute | solution.py:68
  (107 shorter events, 61.5 us)
Async XLA Ops:
  6.5 9.2 %copy-start.1 = (bf16[1,1024,128]{2,1,0:T(8,128)(2,1)S(1)}, bf16[1,1024,128]{2,1,0:T(8,128)(2,1)}, u32[]{:S(2)}) copy-start(bf16[1,1024,128]{2,1,0:T(8,128)(2,1)} %param.15) | copy-start | bytes 786436
  6.5 9.3 %copy-start = (bf16[1,160,1024]{2,1,0:T(8,128)(2,1)S(1)}, bf16[1,160,1024]{2,1,0:T(8,128)(2,1)}, u32[]{:S(2)}) copy-start(bf16[1,160,1024]{2,1,0:T(8,128)(2,1)} %param.11) | copy-start | bytes 983044
  6.5 74.0 %all-gather.11.cloned.1.call-start = ((), (), s32[]{:S(2)}) async-start(), calls=%async_computation.3 | async-start | bytes 2359296 | tf_op jit(solution)/shard_map/all_gather | solution.py:98
  7.3 130.0 %all-gather.13.cloned.1.call-start = ((), (), s32[]{:S(2)}) async-start(), calls=%async_computation.4 | async-start | bytes 2359296 | tf_op jit(solution)/shard_map/all_gather | solution.py:99
  8.0 218.7 %all-gather.15.cloned.1.call-start = ((), (), s32[]{:S(2)}) async-start(), calls=%async_computation.5 | async-start | bytes 2359296 | tf_op jit(solution)/shard_map/all_gather | solution.py:101
  8.7 270.4 %all-gather.17.cloned.1.call-start = ((), (), s32[]{:S(2)}) async-start(), calls=%async_computation.6 | async-start | bytes 4718592 | tf_op jit(solution)/shard_map/all_gather | solution.py:102
  9.3 17.3 %collective-permute-start = (bf16[1024,128]{1,0:T(8,128)(2,1)}, bf16[1024,128]{1,0:T(8,128)(2,1)S(1)}, u32[]{:S(2)}, u32[]{:S(2)}) collective-permute-start(bf16[1024,128]{1,0:T(8,128)(2,1)} %bitcast.176), channel_id=1, source_target_pairs={{0,1},{1,2},{2,3},{3,4},{4,5},{5,6},{6,7},{7,0},{8,9},{9,10},{10,1... | collective-permute-start | bytes 786440 | tf_op jit(solution)/shard_map/ppermute | solution.py:36
  12.3 16.9 %collective-permute-start.1 = (bf16[1024,128]{1,0:T(8,128)(2,1)}, bf16[1024,128]{1,0:T(8,128)(2,1)S(1)}, u32[]{:S(2)}, u32[]{:S(2)}) collective-permute-start(bf16[1024,128]{1,0:T(8,128)(2,1)} %bitcast.177), channel_id=1, source_target_pairs={{0,7},{1,0},{2,1},{3,2},{4,3},{5,4},{6,5},{7,6},{8,15},{9,8},{10,9... | collective-permute-start | bytes 786440 | tf_op jit(solution)/shard_map/ppermute | solution.py:41
  26.6 14.0 %collective-permute-start.2 = (bf16[1024,128]{1,0:T(8,128)(2,1)S(1)}, bf16[1024,128]{1,0:T(8,128)(2,1)S(1)}, u32[]{:S(2)}, u32[]{:S(2)}) collective-permute-start(bf16[1024,128]{1,0:T(8,128)(2,1)S(1)} %collective-permute-done), channel_id=1, source_target_pairs={{0,1},{1,2},{2,3},{3,4},{4,5},{5,6},{6,7},{7,0},{8,9},{9,10},{10,1... | collective-permute-start | bytes 786440 | tf_op jit(solution)/shard_map/ppermute | solution.py:36
  29.3 12.0 %collective-permute-start.3 = (bf16[1024,128]{1,0:T(8,128)(2,1)S(1)}, bf16[1024,128]{1,0:T(8,128)(2,1)S(1)}, u32[]{:S(2)}, u32[]{:S(2)}) collective-permute-start(bf16[1024,128]{1,0:T(8,128)(2,1)S(1)} %collective-permute-done.1), channel_id=1, source_target_pairs={{0,7},{1,0},{2,1},{3,2},{4,3},{5,4},{6,5},{7,6},{8,15},{9,8},{10,9... | collective-permute-start | bytes 786440 | tf_op jit(solution)/shard_map/ppermute | solution.py:41
  40.7 9.2 %collective-permute-start.4 = (bf16[1024,128]{1,0:T(8,128)(2,1)S(1)}, bf16[1024,128]{1,0:T(8,128)(2,1)S(1)}, u32[]{:S(2)}, u32[]{:S(2)}) collective-permute-start(bf16[1024,128]{1,0:T(8,128)(2,1)S(1)} %collective-permute-done.2), channel_id=1, source_target_pairs={{0,1},{1,2},{2,3},{3,4},{4,5},{5,6},{6,7},{7,0},{8,9},{9,10},{10,1... | collective-permute-start | bytes 786440 | tf_op jit(solution)/shard_map/ppermute | solution.py:36
  41.3 17.7 %collective-permute-start.5 = (bf16[1024,128]{1,0:T(8,128)(2,1)S(1)}, bf16[1024,128]{1,0:T(8,128)(2,1)S(1)}, u32[]{:S(2)}, u32[]{:S(2)}) collective-permute-start(bf16[1024,128]{1,0:T(8,128)(2,1)S(1)} %collective-permute-done.3), channel_id=1, source_target_pairs={{0,7},{1,0},{2,1},{3,2},{4,3},{5,4},{6,5},{7,6},{8,15},{9,8},{10,9... | collective-permute-start | bytes 786440 | tf_op jit(solution)/shard_map/ppermute | solution.py:41
  49.9 13.8 %collective-permute-start.6 = (bf16[1024,128]{1,0:T(8,128)(2,1)S(1)}, bf16[1024,128]{1,0:T(8,128)(2,1)S(1)}, u32[]{:S(2)}, u32[]{:S(2)}) collective-permute-start(bf16[1024,128]{1,0:T(8,128)(2,1)S(1)} %collective-permute-done.4), channel_id=1, source_target_pairs={{0,1},{1,2},{2,3},{3,4},{4,5},{5,6},{6,7},{7,0},{8,9},{9,10},{10,1... | collective-permute-start | bytes 786440 | tf_op jit(solution)/shard_map/ppermute | solution.py:36
  83.5 56.9 %all-to-all-start = ((bf16[8,160,128]{2,1,0:T(8,128)(2,1)}), bf16[8,160,128]{2,1,0:T(8,128)(2,1)S(1)}, u32[]{:S(2)}, u32[]{:S(2)}) async-start(bf16[8,160,128]{2,1,0:T(8,128)(2,1)} %bitcast.146), calls=%async_computation | async-start | bytes 655360 | tf_op jit(solution)/shard_map/all_to_all | solution.py:125
  139.4 5.2 %copy-start.3 = (s32[1,8]{1,0:T(1,128)S(1)}, s32[1,8]{1,0:T(1,128)}, u32[]{:S(2)}) copy-start(s32[1,8]{1,0:T(1,128)} %param.12) | copy-start | bytes 100
  139.4 5.7 %copy-start.2 = (bf16[1,31,1024]{2,1,0:T(8,128)(2,1)S(1)}, bf16[1,31,1024]{2,1,0:T(8,128)(2,1)}, u32[]{:S(2)}) copy-start(bf16[1,31,1024]{2,1,0:T(8,128)(2,1)} %param.18) | copy-start | bytes 190468
  140.4 28.9 %all-to-all-start.1 = ((bf16[8,160,256]{2,1,0:T(8,128)(2,1)}), bf16[8,160,256]{2,1,0:T(8,128)(2,1)S(1)}, u32[]{:S(2)}, u32[]{:S(2)}) async-start(bf16[8,160,256]{2,1,0:T(8,128)(2,1)} %maximum_bitcast_fusion), calls=%async_computation.1 | async-start | bytes 1310720 | tf_op jit(solution)/shard_map/all_to_all | solution.py:126
  144.0 186.5 %all-gather.19.cloned.1.call-start = ((), (), s32[]{:S(2)}) async-start(), calls=%async_computation.7 | async-start | bytes 2359296 | tf_op jit(solution)/shard_map/all_gather | solution.py:103
  207.0 19.5 %all-to-all-start.2 = ((bf16[8,160,128]{2,1,0:T(8,128)(2,1)}), bf16[8,160,128]{2,1,0:T(8,128)(2,1)S(1)}, u32[]{:S(2)}, u32[]{:S(2)}) async-start(bf16[8,160,128]{2,1,0:T(8,128)(2,1)} %reshape.468), calls=%async_computation.2 | async-start | bytes 655360 | tf_op jit(solution)/shard_map/all_to_all | solution.py:169
  282.5 4.9 %collective-permute-start.7 = (bf16[15,1024]{1,0:T(8,128)(2,1)S(1)}, bf16[15,1024]{1,0:T(8,128)(2,1)S(1)}, u32[]{:S(2)}, u32[]{:S(2)}) collective-permute-start(bf16[15,1024]{1,0:T(8,128)(2,1)S(1)} %get-tuple-element.84), channel_id=1, source_target_pairs={{0,1},{1,2},{2,3},{3,4},{4,5},{5,6},{6,7},{8,9},{9,10},{10,11},{11... | collective-permute-start | bytes 92168 | tf_op jit(solution)/shard_map/ppermute | solution.py:57
  285.8 6.3 %collective-permute-start.8 = (bf16[15,1024]{1,0:T(8,128)(2,1)S(1)}, bf16[15,1024]{1,0:T(8,128)(2,1)S(1)}, u32[]{:S(2)}, u32[]{:S(2)}) collective-permute-start(bf16[15,1024]{1,0:T(8,128)(2,1)S(1)} %get-tuple-element.85), channel_id=1, source_target_pairs={{1,0},{2,1},{3,2},{4,3},{5,4},{6,5},{7,6},{9,8},{10,9},{11,10},{12... | collective-permute-start | bytes 92168 | tf_op jit(solution)/shard_map/ppermute | solution.py:60
  332.7 6.6 %collective-permute-start.9 = (bf16[160,1024]{1,0:T(8,128)(2,1)S(1)}, bf16[160,1024]{1,0:T(8,128)(2,1)S(1)}, u32[]{:S(2)}, u32[]{:S(2)}) collective-permute-start(bf16[160,1024]{1,0:T(8,128)(2,1)S(1)} %fusion.51), channel_id=1, source_target_pairs={{24,0},{0,8},{8,16},{16,24},{25,1},{1,9},{9,17},{17,25},{26,2},{2,... | collective-permute-start | bytes 983048 | tf_op jit(solution)/shard_map/ppermute | solution.py:68
Sparse Core Ops, SparseCore 0:
  9.4 71.0 all-gather.10
  82.6 54.5 all-gather.12
  139.3 57.6 all-gather.14
  198.8 80.2 all-gather.16
  281.1 49.3 all-gather.18
